TPU v7x, 32 devices: a whole 2x2x4 slice. The times are simulated.
32 devices in a mesh: groups: 2 (over x), expert: 16 (over z, y, core).
Axes of the slice: x: 2, y: 2, z: 4, core: 2. Of those that a mesh axis runs over, the one named last changes fastest.
Arguments:
- activations: bfloat16 [64, 6144], P(('groups', 'expert')), parts along dimension 0, may hold values from -6 to 6
- out_grads: bfloat16 [64, 6144], P(('groups', 'expert')), parts along dimension 0, may hold values from -6 to 6
- expert_ids: int32 [64, 4], P(('groups', 'expert')), parts along dimension 0, may hold values from 0 to 15, all different within a row; in each aligned block of 2 rows (0 to 1, 2 to 3, ...) at most 2 rows name the same one
- route_scores: float32 [64, 4], P(('groups', 'expert')), parts along dimension 0, may hold values from 0.05 to 1
- w_gate: bfloat16 [43008, 6144], P('expert'), may hold values from -0.078125 to 0.078125
- w_up: bfloat16 [43008, 6144], P('expert'), may hold values from -0.078125 to 0.078125
Outputs:
- fisher: bfloat16 [86016, 6144], P(('groups', 'expert')), parts along dimension 0
There are 2 independent parts, one for each index of `groups`. A program takes and returns all parts, laid end to end along the dimension named above; an argument that names none is the same for every part. Nothing has to cross between parts.
Inputs may be any that keep to these rules, and one draw needn't show every extreme that they name: `expert_ids`: each row names 4 different experts; every expert is named somewhere; in the rows of one device no expert is named by more than 2 rows, a bound that some block reaches.
All inputs are finite; a program needn't handle non-finite values.
Results may differ from a plain program's by a relative error of at most 0.0091.
Values may be sent and summed in bfloat16 or wider, within the bound.
A program may use at most 320 MiB of HBM per device.

v0:
```python
import jax
import jax.numpy as jnp
from jax import lax
from jax.sharding import PartitionSpec as P

D = 6144
FF = 10752
EXPERTS = 4


def fisher_term(rows, scaled, gate_rows, up_rows):
    dims = (((1,), (1,)), ((), ()))
    gate = lax.dot_general(rows, gate_rows, dims, preferred_element_type=jnp.float32)
    upper = lax.dot_general(rows, up_rows, dims, preferred_element_type=jnp.float32)
    hidden = jax.nn.silu(gate) * upper
    hidden_sq = (hidden * hidden).astype(jnp.bfloat16)
    grad32 = scaled.astype(jnp.float32)
    grad_sq = (grad32 * grad32).astype(jnp.bfloat16)
    return lax.dot_general(
        hidden_sq, grad_sq, (((0,), (0,)), ((), ())), preferred_element_type=jnp.float32
    )


def per_device(activations, out_grads, expert_ids, route_scores, w_gate, w_up):
    devices = lax.axis_size("expert")
    shards = devices // EXPERTS
    share = route_scores / jnp.sum(route_scores, axis=1, keepdims=True)
    columns = jnp.arange(EXPERTS, dtype=jnp.int32)
    matches = expert_ids[:, :, None] == columns[None, None, :]
    picked = matches.astype(jnp.float32)
    weight = jnp.sum(picked * share[:, :, None], axis=1).astype(jnp.bfloat16)
    tok_rows = activations.shape[0]
    width = activations.shape[1]
    per_expert = (
        jnp.transpose(weight).astype(jnp.float32)[:, :, None] * out_grads.astype(jnp.float32)[None]
    ).astype(jnp.bfloat16)
    grad_send = jnp.repeat(per_expert, shards, axis=0)
    rows_send = jnp.broadcast_to(activations[None], (devices, tok_rows, width))
    rows_recv, grad_recv = (
        lax.all_to_all(rows_send, "expert", split_axis=0, concat_axis=0, tiled=True),
        lax.all_to_all(grad_send, "expert", split_axis=0, concat_axis=0, tiled=True),
    )
    raw = fisher_term(
        rows_recv.reshape(devices * tok_rows, width),
        grad_recv.reshape(devices * tok_rows, width),
        w_gate,
        w_up,
    )
    total = lax.psum(jnp.sum(raw), "expert")
    return (raw * (EXPERTS * FF * D / total)).astype(jnp.bfloat16)


def solution(mesh):
    return jax.shard_map(
        per_device,
        mesh=mesh,
        in_specs=(
            P(("groups", "expert"), None),
            P(("groups", "expert"), None),
            P(("groups", "expert"), None),
            P(("groups", "expert"), None),
            P("expert", None),
            P("expert", None),
        ),
        out_specs=P(("groups", "expert"), None),
        check_vma=False,
    )
```

profile of v0, /device:TPU:0, one launch (start us, length us, event | category | flops | bytes accessed | tf_op | source)
XLA Modules:
  0.0 160.9 jit_solution(11276296878059557871)
XLA Ops:
  0.0 0.8 reduce_sum.27
  0.8 0.7 broadcast_divide_fusion
  1.5 0.8 select_reduce_fusion
  2.3 0.1 copy.8
  2.4 0.8 convert_element_type.38
  3.2 0.1 multiply_convert_fusion.2
  3.3 0.2 broadcast_in_dim.5
  3.5 19.4 %all_to_all.10 = bf16[16,2,6144]{2,1,0:T(2,128)(2,1)S(1)} all-to-all(bf16[16,2,6144]{2,1,0:T(2,128)(2,1)S(1)} %bitcast.8), channel_id=1, replica_groups=mesh['groups'=2,'expert'=16] {'expert'}, dimensions={0} | all-to-all | bytes 786432 | tf_op jit(solution)/shard_map/all_to_all | solution.py:41
  22.9 1.7 %broadcast_in_dim.4 = bf16[16,2,6144]{2,1,0:T(2,128)(2,1)} broadcast(bf16[2,6144]{1,0:T(2,128)(2,1)} %param.6), dimensions={1,2} | broadcast | bytes 417792 | tf_op jit(solution)/shard_map/broadcast_in_dim | solution.py:38
  24.6 3.6 %all-to-all-start = ((bf16[16,2,6144]{2,1,0:T(2,128)(2,1)}), bf16[16,2,6144]{2,1,0:T(2,128)(2,1)S(1)}, u32[]{:S(2)}, u32[]{:S(2)}) async-start(bf16[16,2,6144]{2,1,0:T(2,128)(2,1)} %broadcast_in_dim.4), calls=%async_computation | async-start | bytes 786432 | tf_op jit(solution)/shard_map/all_to_all | solution.py:40
  28.2 0.3 multiply_convert_fusion.1
  28.5 0.1 convert_element_type.42
  28.6 11.7 %all-to-all-done = bf16[16,2,6144]{2,1,0:T(2,128)(2,1)S(1)} async-done(((bf16[16,2,6144]{2,1,0:T(2,128)(2,1)}), bf16[16,2,6144]{2,1,0:T(2,128)(2,1)S(1)}, u32[]{:S(2)}, u32[]{:S(2)}) %all-to-all-start) | async-done | bytes 393248 | tf_op jit(solution)/shard_map/all_to_all | solution.py:40
  40.3 0.1 reshape.16
  40.5 15.0 %fusion.11 = f32[32,2688]{1,0:T(8,128)S(1)} fusion(bf16[32,6144]{1,0:T(8,128)(2,1)S(1)} %reshape.16, bf16[2688,6144]{1,0:T(8,128)(2,1)} %param.10), kind=kOutput, calls=%fused_computation.19 | convolution fusion | flops 1056964608 | bytes 33767424 | tf_op jit(solution)/shard_map/dot_general | solution.py:13
  55.5 40.7 %fusion.10 = (f32[]{:T(128)}, f32[2688,6144]{1,0:T(8,128)}) fusion(bf16[32,6144]{1,0:T(8,128)(2,1)S(1)} %convert_element_type.42, bf16[32,6144]{1,0:T(8,128)(2,1)S(1)} %reshape.16, bf16[2688,6144]{1,0:T(8,128)(2,1)} %param.11, f32[32,2688]{1,0:T(8,128)S(1)} %fusion.11), kind=kOutput, calls=%fused_computation.18 | convolution fusion | flops 2131046400 | bytes 100220928 | tf_op jit(solution)/shard_map/dot_general | solution.py:19
  96.2 32.1 %psum.7 = f32[]{:T(128)} all-reduce(f32[]{:T(128)} %get-tuple-element.5), channel_id=1, replica_groups=mesh['groups'=2,'expert'=16] {'expert'}, use_global_device_ids=true, to_apply=%region_3.4 | all-reduce | flops 1 | bytes 8 | tf_op jit(solution)/shard_map/psum | solution.py:49
  129.0 31.9 %multiply_convert_fusion = bf16[2688,6144]{1,0:T(8,128)(2,1)} fusion(f32[2688,6144]{1,0:T(8,128)} %get-tuple-element.6, f32[]{:T(128)S(6)} %div.18), kind=kLoop, calls=%fused_computation | loop fusion | flops 33030144 | bytes 99090432 | tf_op jit(solution)/shard_map/convert_element_type | solution.py:50
  (1 shorter events, 0.0 us)
Async XLA Ops:
  24.6 15.7 %all-to-all-start = ((bf16[16,2,6144]{2,1,0:T(2,128)(2,1)}), bf16[16,2,6144]{2,1,0:T(2,128)(2,1)S(1)}, u32[]{:S(2)}, u32[]{:S(2)}) async-start(bf16[16,2,6144]{2,1,0:T(2,128)(2,1)} %broadcast_in_dim.4), calls=%async_computation | async-start | bytes 786432 | tf_op jit(solution)/shard_map/all_to_all | solution.py:40
where the time goes:
time: 162 us; the launch traced here: 161 us
  matrix products  55.7 us (34%)
  blocking collectives  51.5 us (32%)
  other arithmetic  35.5 us (22%)
  waiting for transfers between devices  11.7 us (7%)
  starting transfers between devices  3.55 us (2%)
  local copies, waits for them, and re-layouts  2.29 us (1%)
    dot_general x1, matrix products, fisher_term(): lax.dot_general(hidden_sq, grad_sq, (((0,), (0,)), ((), ())), preferred_e...  40.7 us
    psum x1, blocking collectives, per_device(): total = lax.psum(jnp.sum(raw), 'expert')  32.1 us
    convert_element_type x1, other arithmetic, per_device(): return (raw * (EXPERTS * FF * D / total)).astype(jnp.bfloat16)  31.9 us
    all_to_all x1, blocking collectives, per_device(): lax.all_to_all(grad_send, 'expert', split_axis=0, concat_axis=0, tiled=True)  19.4 us
    dot_general x1, matrix products, fisher_term(): lax.dot_general(rows, gate_rows, dims, preferred_element_type=jnp.float32)  15 us
    all_to_all x1, waiting for transfers between devices, per_device(): lax.all_to_all(rows_send, 'expert', split_axis=0, concat_axis=0, tiled=True)  11.7 us
    all_to_all x1, starting transfers between devices, per_device(): lax.all_to_all(rows_send, 'expert', split_axis=0, concat_axis=0, tiled=True)  3.55 us
  transfers between devices with their start and end apart: 1, of which 1 were waited for; matrix products, arithmetic and copies ran while one was open for 0% of the time, Pallas kernels for 0%

commit v1 on v0

v1 whole, which is shorter than its diff:
```python
import functools

import jax
import jax.numpy as jnp
from jax import lax
from jax.experimental import pallas as pl
from jax.experimental.pallas import tpu as pltpu
from jax.sharding import PartitionSpec as P

EXPERTS = 4
LANES = 128
MESH = pl.DeviceIdType.MESH
NT = (((1,), (1,)), ((), ()))


def chunk_of(rows, most):
    best = 16
    for size in range(16, most + 1, 16):
        if rows % size == 0:
            best = size
    return best


def hidden_kernel(
    devices, chunk, slots, first,
    gate_ref, up_ref, act_ref, grad_ref, ids_ref, score_ref,
    hsq_ref, gsq_ref, scale_ref,
    wbuf, stage, wide, abuf, gsend, gbuf, acts, sums, pbuf,
    wsem, a_send, a_recv, g_send, g_recv, p_send, p_recv,
):
    group = lax.axis_index("groups")
    me = lax.axis_index("expert")
    chips = devices // 2
    chip, core = me // 2, me % 2
    twin = chip * 2 + (1 - core)
    rows, width = gate_ref.shape
    chunks = rows // chunk
    segments = width // LANES
    tok_rows = act_ref.shape[0]
    tokens = devices * tok_rows
    block = tok_rows * segments

    def weights(index, slot):
        span = pl.ds(pl.multiple_of(index * chunk, chunk), chunk)
        return (
            pltpu.make_async_copy(gate_ref.at[span], wbuf.at[slot, pl.ds(0, chunk)], wsem.at[slot, 0]),
            pltpu.make_async_copy(up_ref.at[span], wbuf.at[slot, pl.ds(chunk, chunk)], wsem.at[slot, 1]),
        )

    def remote(src, dst, send, recv, to):
        return pltpu.make_async_remote_copy(
            src_ref=src, dst_ref=dst, send_sem=send, recv_sem=recv,
            device_id=(group, to), device_id_type=MESH,
        )

    def each(low, high, body):
        lax.fori_loop(low, high, lambda i, c: (body(i), c)[1], 0)

    def start_weights(i):
        for copy in weights(i, i):
            copy.start()

    each(0, slots, start_weights)

    barrier = pltpu.get_barrier_semaphore()

    def greet(k):
        pl.semaphore_signal(
            barrier, inc=1, device_id=(group, lax.rem(me + k, devices)), device_id_type=MESH
        )

    each(1, devices, greet)

    def to_rows(value):
        for seg in range(segments):
            stage[pl.ds(seg, tok_rows, stride=segments), :] = value[:, seg * LANES:(seg + 1) * LANES]
        return stage[...]

    abuf[me] = to_rows(act_ref[...].astype(jnp.float32)).astype(jnp.bfloat16)
    pl.semaphore_wait(barrier, devices - 1)

    def peer(k):
        return lax.rem(chip + k, chips) * 2 + core

    def act_copy(k):
        return remote(abuf.at[me], abuf.at[me], a_send.at[k], a_recv.at[me], peer(k))

    def act_forward(k):
        source = peer(k)
        return remote(abuf.at[source], abuf.at[source], a_send.at[chips + k], a_recv.at[source], twin)

    act_forward(0).start()
    each(1, chips, lambda k: act_copy(k).start())

    score = score_ref[...]
    share = score / jnp.sum(score, axis=1, keepdims=True)
    ids = ids_ref[...]
    grad = to_rows(grad_ref[...].astype(jnp.float32))
    row_token = lax.broadcasted_iota(jnp.int32, (block, 1), 0) // segments
    for index in range(EXPERTS):
        weight = jnp.sum(jnp.where(ids == index, share, 0.0), axis=1, keepdims=True)
        weight = weight.astype(jnp.bfloat16).astype(jnp.float32)
        spread = jnp.zeros((block, 1), jnp.float32)
        for token in range(tok_rows):
            spread = jnp.where(row_token == token, weight[token:token + 1, :], spread)
        scaled = (grad * spread).astype(jnp.bfloat16).astype(jnp.float32)
        gsend[index] = (scaled * scaled).astype(jnp.bfloat16)
    gbuf[me] = gsend[me // (devices // EXPERTS)]

    def grad_copy(k):
        to = peer(k)
        return remote(gsend.at[to // (devices // EXPERTS)], gbuf.at[me], g_send.at[k], g_recv.at[me], to)

    def grad_forward(k):
        source = peer(k)
        return remote(gbuf.at[source], gbuf.at[source], g_send.at[chips + k], g_recv.at[source], twin)

    def pass_on(copy, forward):
        def one(k):
            source = lax.rem(chip - k + chips, chips) * 2 + core
            remote(abuf.at[me], abuf.at[source], a_send.at[k], copy.at[source], twin).wait_recv()
            forward(lax.rem(chips - k, chips)).start()

        each(1, chips, one)

    def from_twin(recv):
        def one(k):
            source = k * 2 + (1 - core)
            remote(abuf.at[me], abuf.at[source], a_send.at[0], recv.at[source], twin).wait_recv()

        each(0, chips, one)

    pass_on(a_recv, act_forward)
    grad_forward(0).start()
    each(1, chips, lambda k: grad_copy(k).start())
    from_twin(a_recv)

    def to_tokens(source, target):
        wide[...] = source[...].astype(jnp.float32).reshape(devices * block, LANES)
        total = jnp.zeros((tokens, LANES), jnp.float32)
        for seg in range(segments):
            piece = wide[pl.ds(seg, tokens, stride=segments), :]
            target[:, seg * LANES:(seg + 1) * LANES] = piece.astype(jnp.bfloat16)
            total = total + piece
        return total

    to_tokens(abuf, acts)
    sums[...] = jnp.zeros_like(sums)

    def hidden(index):
        slot = lax.rem(index, slots)
        for copy in weights(index, slot):
            copy.wait()
        both = lax.dot_general(wbuf[slot], acts[...], NT, preferred_element_type=jnp.float32)

        @pl.when(index + slots < chunks)
        def _():
            for copy in weights(index + slots, slot):
                copy.start()

        gate, upper = both[:chunk], both[chunk:]
        value = gate / (1.0 + jnp.exp(-gate)) * upper
        square = (value * value).astype(jnp.bfloat16)
        hsq_ref[pl.ds(pl.multiple_of(index * chunk, chunk), chunk), :] = square
        sums[...] += jnp.sum(square.astype(jnp.float32), axis=0, keepdims=True)

    each(0, first, hidden)
    pass_on(g_recv, grad_forward)
    from_twin(g_recv)
    grad_sum = jnp.sum(to_tokens(gbuf, gsq_ref), axis=1, keepdims=True)
    each(first, chunks, hidden)

    same = lax.broadcasted_iota(jnp.int32, (tokens, tokens), 0) == lax.broadcasted_iota(
        jnp.int32, (tokens, tokens), 1
    )
    column = jnp.sum(jnp.where(same, sums[...], 0.0), axis=1, keepdims=True)
    part = jnp.sum(column * grad_sum, axis=0, keepdims=True)
    pbuf[me] = jnp.broadcast_to(part, (8, LANES))

    def part_copy(k):
        return remote(pbuf.at[me], pbuf.at[me], p_send.at[k], p_recv.at[me], lax.rem(me + k, devices))

    each(1, devices, lambda k: part_copy(k).start())

    def part_wait(k):
        source = lax.rem(me + k, devices)
        remote(pbuf.at[me], pbuf.at[source], p_send.at[k], p_recv.at[source], source).wait_recv()

    each(1, devices, part_wait)
    total = jnp.sum(pbuf[...], axis=0)
    scale_ref[...] = (float(devices) * rows * width) / total

    def drain(k):
        act_copy(k).wait_send()
        act_forward(k).wait_send()
        grad_copy(k).wait_send()
        grad_forward(k).wait_send()

    act_forward(0).wait_send()
    grad_forward(0).wait_send()
    each(1, chips, drain)
    each(1, devices, lambda k: part_copy(k).wait_send())


def outer_kernel(tile, hsq_ref, gsq_ref, scale_ref, out_ref):
    scale = scale_ref[0:1, 0:1]
    left = hsq_ref[...]
    for start in range(0, out_ref.shape[1], tile):
        span = slice(start, start + tile)
        raw = jnp.dot(left, gsq_ref[:, span], preferred_element_type=jnp.float32)
        out_ref[:, span] = (raw * scale).astype(jnp.bfloat16)


def per_device(activations, out_grads, expert_ids, route_scores, w_gate, w_up):
    devices = lax.axis_size("expert")
    rows, width = w_gate.shape
    tok_rows = activations.shape[0]
    tokens = devices * tok_rows
    segments = width // LANES
    block = tok_rows * segments
    chunk = chunk_of(rows, 128)
    chunks = rows // chunk
    slots = min(12, chunks)
    chips = devices // 2
    vmem = pl.BlockSpec(memory_space=pltpu.VMEM)
    anywhere = pl.BlockSpec(memory_space=pl.ANY)
    dma = pltpu.SemaphoreType.DMA
    bf16, f32 = jnp.bfloat16, jnp.float32
    hsq, gsq, scale = pl.pallas_call(
        functools.partial(hidden_kernel, devices, chunk, slots, chunks // 3),
        out_shape=(
            jax.ShapeDtypeStruct((rows, tokens), bf16),
            jax.ShapeDtypeStruct((tokens, width), bf16),
            jax.ShapeDtypeStruct((8, LANES), f32),
        ),
        in_specs=[anywhere, anywhere, vmem, vmem, vmem, vmem],
        out_specs=(vmem, vmem, vmem),
        scratch_shapes=[
            pltpu.VMEM((slots, 2 * chunk, width), bf16),
            pltpu.VMEM((block, LANES), f32),
            pltpu.VMEM((devices * block, LANES), f32),
            pltpu.VMEM((devices, block, LANES), bf16),
            pltpu.VMEM((EXPERTS, block, LANES), bf16),
            pltpu.VMEM((devices, block, LANES), bf16),
            pltpu.VMEM((tokens, width), bf16),
            pltpu.VMEM((1, tokens), f32),
            pltpu.VMEM((devices, 8, LANES), f32),
            dma((slots, 2)),
            dma((2 * chips,)),
            dma((devices,)),
            dma((2 * chips,)),
            dma((devices,)),
            dma((devices,)),
            dma((devices,)),
        ],
        compiler_params=pltpu.CompilerParams(
            collective_id=0, has_side_effects=True, vmem_limit_bytes=56 * 1024 * 1024
        ),
        cost_estimate=pl.CostEstimate(
            flops=4 * rows * width * tokens, bytes_accessed=4 * rows * width, transcendentals=rows * tokens
        ),
    )(w_gate, w_up, activations, out_grads, expert_ids, route_scores)

    height = chunk_of(rows, 256)
    return pl.pallas_call(
        functools.partial(outer_kernel, 512),
        out_shape=jax.ShapeDtypeStruct((rows, width), bf16),
        grid=(rows // height,),
        in_specs=[
            pl.BlockSpec((height, tokens), lambda i: (i, 0)),
            pl.BlockSpec((tokens, width), lambda i: (0, 0)),
            pl.BlockSpec((8, LANES), lambda i: (0, 0)),
        ],
        out_specs=pl.BlockSpec((height, width), lambda i: (i, 0)),
        compiler_params=pltpu.CompilerParams(vmem_limit_bytes=48 * 1024 * 1024),
        cost_estimate=pl.CostEstimate(
            flops=2 * rows * width * tokens, bytes_accessed=2 * rows * width, transcendentals=0
        ),
    )(hsq, gsq, scale)


def solution(mesh):
    return jax.shard_map(
        per_device,
        mesh=mesh,
        in_specs=(
            P(("groups", "expert"), None),
            P(("groups", "expert"), None),
            P(("groups", "expert"), None),
            P(("groups", "expert"), None),
            P("expert", None),
            P("expert", None),
        ),
        out_specs=P(("groups", "expert"), None),
        check_vma=False,
    )
```

time: 162 us -> 61.5 us (0.38)
  Pallas kernels: 0 us -> 58.4 us
  matrix products: 55.7 us -> 0 us
  blocking collectives: 51.5 us -> 0 us
  other arithmetic: 35.5 us -> 0 us
  waiting for transfers between devices: 11.7 us -> 0 us
  starting transfers between devices: 3.55 us -> 0 us
    pallas_call x0 -> x2, Pallas kernels: none -> 58.4 us  [the longest x1 43.2 us: per_device(): pl.pallas_call(functools.partial(hidden_kernel, devices, chunk, slots, ch...]
    dot_general x2 -> x0, matrix products: 55.7 us -> none  [the longest x1 40.7 us: fisher_term(): lax.dot_general(hidden_sq, grad_sq, (((0,), (0,)), ((), ())), preferred_e...]
    convert_element_type x5 -> x0, other arithmetic: 33.1 us -> none  [the longest x1 31.9 us: per_device(): return (raw * (EXPERTS * FF * D / total)).astype(jnp.bfloat16)]
    psum x1 -> x0, blocking collectives: 32.1 us -> none  [per_device(): total = lax.psum(jnp.sum(raw), 'expert')]
    all_to_all x1 -> x0, blocking collectives: 19.4 us -> none  [per_device(): lax.all_to_all(grad_send, 'expert', split_axis=0, concat_axis=0, tiled=True)]
    all_to_all x1 -> x0, waiting for transfers between devices: 11.7 us -> none  [per_device(): lax.all_to_all(rows_send, 'expert', split_axis=0, concat_axis=0, tiled=True)]
    all_to_all x1 -> x0, starting transfers between devices: 3.55 us -> none  [per_device(): lax.all_to_all(rows_send, 'expert', split_axis=0, concat_axis=0, tiled=True)]
    unnamed x0 -> x6, local copies, waits for them, and re-layouts: none -> 2.76 us
  transfers between devices with their start and end apart: 1 -> 0, of which waited for: 1 -> 0; matrix products, arithmetic and copies ran while one was open for 0% -> 0% of each run, Pallas kernels for 0% -> 0%
where the time goes in v1:
time: 61.5 us; the launch traced here: 61.2 us
  Pallas kernels  58.4 us (95%)
  local copies, waits for them, and re-layouts  2.76 us (4%)
    pallas_call x1, Pallas kernels, per_device(): pl.pallas_call(functools.partial(hidden_kernel, devices, chunk, slots, ch...  43.2 us
    pallas_call x1, Pallas kernels, per_device(): pl.pallas_call(functools.partial(outer_kernel, 512), out_shape=jax.ShapeD...  15.2 us
    unnamed x6, local copies, waits for them, and re-layouts  2.76 us

profile of v1, /device:TPU:0, one launch (start us, length us, event | category | flops | bytes accessed | tf_op | source)
XLA Modules:
  0.0 61.2 jit_solution(221570463040501849)
XLA Ops:
  0.0 43.2 %shard_map.64 = (bf16[2688,32]{1,0:T(8,128)(2,1)}, bf16[32,6144]{1,0:T(8,128)(2,1)}, f32[8,128]{1,0:T(8,128)}) custom-call(bf16[2688,6144]{1,0:T(8,128)(2,1)} %gate_ref.1, bf16[2688,6144]{1,0:T(8,128)(2,1)} %up_ref.1, bf16[2,6144]{1,0:T(2,128)(2,1)} %act_ref.1, bf16[2,6144]{1,0:T(2,128)(2,1)} %grad_ref.1, s32[2,4]{1,0:T(2,128)} %ids_ref.1, f32[2,4]{1,0:T(2,128)} %score_ref.1), custom_call_target="tpu_custom_call" | custom-call | flops 2113929216 | bytes 66060288 | tf_op jit(solution)/shard_map/pallas_call | solution.py:229
  43.2 0.0 copy-start
  43.2 1.1 %copy-done = bf16[2688,32]{1,0:T(8,128)(2,1)S(1)} copy-done((bf16[2688,32]{1,0:T(8,128)(2,1)S(1)}, bf16[2688,32]{1,0:T(8,128)(2,1)}, u32[]{:S(2)}) %copy-start) | copy-done | bytes 172056
  44.3 0.0 copy-start.1
  44.3 1.0 %copy-done.1 = bf16[32,6144]{1,0:T(8,128)(2,1)S(1)} copy-done((bf16[32,6144]{1,0:T(8,128)(2,1)S(1)}, bf16[32,6144]{1,0:T(8,128)(2,1)}, u32[]{:S(2)}) %copy-start.1) | copy-done | bytes 393240
  45.3 0.0 copy-start.2
  45.3 0.7 %copy-done.2 = f32[8,128]{1,0:T(8,128)S(1)} copy-done((f32[8,128]{1,0:T(8,128)S(1)}, f32[8,128]{1,0:T(8,128)}, u32[]{:S(2)}) %copy-start.2) | copy-done | bytes 4120
  46.0 15.2 %shard_map.65 = bf16[2688,6144]{1,0:T(8,128)(2,1)} custom-call(bf16[2688,32]{1,0:T(8,128)(2,1)S(1)} %copy-done, bf16[32,6144]{1,0:T(8,128)(2,1)S(1)} %copy-done.1, f32[8,128]{1,0:T(8,128)S(1)} %copy-done.2), custom_call_target="tpu_custom_call" | custom-call | flops 1056964608 | bytes 33030144 | tf_op jit(solution)/shard_map/pallas_call | solution.py:265
Async XLA Ops:
  43.2 1.1 %copy-start = (bf16[2688,32]{1,0:T(8,128)(2,1)S(1)}, bf16[2688,32]{1,0:T(8,128)(2,1)}, u32[]{:S(2)}) copy-start(bf16[2688,32]{1,0:T(8,128)(2,1)} %get-tuple-element.8.hsq_ref) | copy-start | bytes 516100
  44.3 1.0 %copy-start.1 = (bf16[32,6144]{1,0:T(8,128)(2,1)S(1)}, bf16[32,6144]{1,0:T(8,128)(2,1)}, u32[]{:S(2)}) copy-start(bf16[32,6144]{1,0:T(8,128)(2,1)} %get-tuple-element.9.gsq_ref) | copy-start | bytes 1179652
  45.3 0.7 %copy-start.2 = (f32[8,128]{1,0:T(8,128)S(1)}, f32[8,128]{1,0:T(8,128)}, u32[]{:S(2)}) copy-start(f32[8,128]{1,0:T(8,128)} %get-tuple-element.10.scale_ref) | copy-start | bytes 12292

commit v2 on v1

--- a/solution.py
+++ b/solution.py
@@ -60,7 +60,8 @@
         for copy in weights(i, i):
             copy.start()
 
-    each(0, slots, start_weights)
+    early, middle = min(2, slots), min(5, slots)
+    each(0, early, start_weights)
 
     barrier = pltpu.get_barrier_semaphore()
 
@@ -130,7 +131,9 @@
 
         each(0, chips, one)
 
+    each(early, middle, start_weights)
     pass_on(a_recv, act_forward)
+    each(middle, slots, start_weights)
     grad_forward(0).start()
     each(1, chips, lambda k: grad_copy(k).start())
     from_twin(a_recv)
@@ -204,7 +207,8 @@
 
 def outer_kernel(tile, hsq_ref, gsq_ref, scale_ref, out_ref):
     scale = scale_ref[0:1, 0:1]
-    left = hsq_ref[...]
+    height = out_ref.shape[0]
+    left = hsq_ref[pl.ds(pl.multiple_of(pl.program_id(0) * height, height), height), :]
     for start in range(0, out_ref.shape[1], tile):
         span = slice(start, start + tile)
         raw = jnp.dot(left, gsq_ref[:, span], preferred_element_type=jnp.float32)
@@ -220,7 +224,7 @@
     block = tok_rows * segments
     chunk = chunk_of(rows, 128)
     chunks = rows // chunk
-    slots = min(12, chunks)
+    slots = min(10, chunks)
     chips = devices // 2
     vmem = pl.BlockSpec(memory_space=pltpu.VMEM)
     anywhere = pl.BlockSpec(memory_space=pl.ANY)
@@ -254,25 +258,25 @@
             dma((devices,)),
         ],
         compiler_params=pltpu.CompilerParams(
-            collective_id=0, has_side_effects=True, vmem_limit_bytes=56 * 1024 * 1024
+            collective_id=0, has_side_effects=True, vmem_limit_bytes=44 * 1024 * 1024
         ),
         cost_estimate=pl.CostEstimate(
             flops=4 * rows * width * tokens, bytes_accessed=4 * rows * width, transcendentals=rows * tokens
         ),
     )(w_gate, w_up, activations, out_grads, expert_ids, route_scores)
 
-    height = chunk_of(rows, 256)
+    height = chunk_of(rows, 384)
     return pl.pallas_call(
-        functools.partial(outer_kernel, 512),
+        functools.partial(outer_kernel, 256),
         out_shape=jax.ShapeDtypeStruct((rows, width), bf16),
         grid=(rows // height,),
         in_specs=[
-            pl.BlockSpec((height, tokens), lambda i: (i, 0)),
-            pl.BlockSpec((tokens, width), lambda i: (0, 0)),
-            pl.BlockSpec((8, LANES), lambda i: (0, 0)),
+            vmem,
+            vmem,
+            vmem,
         ],
         out_specs=pl.BlockSpec((height, width), lambda i: (i, 0)),
-        compiler_params=pltpu.CompilerParams(vmem_limit_bytes=48 * 1024 * 1024),
+        compiler_params=pltpu.CompilerParams(vmem_limit_bytes=20 * 1024 * 1024),
         cost_estimate=pl.CostEstimate(
             flops=2 * rows * width * tokens, bytes_accessed=2 * rows * width, transcendentals=0
         ),

time: 61.5 us -> 58.5 us (0.951)
  Pallas kernels: 58.4 us -> 55.4 us
    pallas_call x1, Pallas kernels: 43.2 us -> 41.2 us  [per_device(): pl.pallas_call(functools.partial(hidden_kernel, devices, chunk, slots, ch...]
    pallas_call x1, Pallas kernels: 15.2 us -> 14.2 us  [per_device(): pl.pallas_call(functools.partial(outer_kernel, 256), out_shape=jax.ShapeD...]
    unnamed x6 -> x8, local copies, waits for them, and re-layouts: 2.76 us -> 2.83 us
where the time goes in v2:
time: 58.5 us; the launch traced here: 58.3 us
  Pallas kernels  55.4 us (95%)
  local copies, waits for them, and re-layouts  2.83 us (5%)
    pallas_call x1, Pallas kernels, per_device(): pl.pallas_call(functools.partial(hidden_kernel, devices, chunk, slots, ch...  41.2 us
    pallas_call x1, Pallas kernels, per_device(): pl.pallas_call(functools.partial(outer_kernel, 256), out_shape=jax.ShapeD...  14.2 us
    unnamed x8, local copies, waits for them, and re-layouts  2.83 us

profile of v2, /device:TPU:0, one launch (start us, length us, event | category | flops | bytes accessed | tf_op | source)
XLA Modules:
  0.0 58.3 jit_solution(4942687001178679575)
XLA Ops:
  0.0 0.0 copy-start
  0.0 0.7 %copy-done = bf16[2,6144]{1,0:T(2,128)(2,1)S(1)} copy-done((bf16[2,6144]{1,0:T(2,128)(2,1)S(1)}, bf16[2,6144]{1,0:T(2,128)(2,1)}, u32[]{:S(2)}) %copy-start) | copy-done | bytes 24600
  0.7 0.0 copy-start.1
  0.7 0.7 %copy-done.1 = bf16[2,6144]{1,0:T(2,128)(2,1)S(1)} copy-done((bf16[2,6144]{1,0:T(2,128)(2,1)S(1)}, bf16[2,6144]{1,0:T(2,128)(2,1)}, u32[]{:S(2)}) %copy-start.1) | copy-done | bytes 24600
  1.5 0.0 copy-start.2
  1.5 0.7 %copy-done.2 = s32[2,4]{1,0:T(2,128)S(1)} copy-done((s32[2,4]{1,0:T(2,128)S(1)}, s32[2,4]{1,0:T(2,128)}, u32[]{:S(2)}) %copy-start.2) | copy-done | bytes 56
  2.2 0.0 copy-start.3
  2.2 0.7 %copy-done.3 = f32[2,4]{1,0:T(2,128)S(1)} copy-done((f32[2,4]{1,0:T(2,128)S(1)}, f32[2,4]{1,0:T(2,128)}, u32[]{:S(2)}) %copy-start.3) | copy-done | bytes 56
  2.8 41.2 %shard_map.64 = (bf16[2688,32]{1,0:T(8,128)(2,1)S(1)}, bf16[32,6144]{1,0:T(8,128)(2,1)S(1)}, f32[8,128]{1,0:T(8,128)S(1)}) custom-call(bf16[2688,6144]{1,0:T(8,128)(2,1)} %gate_ref.1, bf16[2688,6144]{1,0:T(8,128)(2,1)} %up_ref.1, bf16[2,6144]{1,0:T(2,128)(2,1)S(1)} %copy-done, bf16[2,6144]{1,0:T(2,128)(2,1)S(1)} %copy-done.1, s32[2,4]{1,0:T(2,128)S(1)} %copy-done.2, ...), custom_call_target="tpu_custom_call" | custom-call | flops 2113929216 | bytes 66060288 | tf_op jit(solution)/shard_map/pallas_call | solution.py:233
  44.1 14.2 %shard_map.65 = bf16[2688,6144]{1,0:T(8,128)(2,1)} custom-call(bf16[2688,32]{1,0:T(8,128)(2,1)S(1)} %get-tuple-element.8.hsq_ref, bf16[32,6144]{1,0:T(8,128)(2,1)S(1)} %get-tuple-element.9.gsq_ref, f32[8,128]{1,0:T(8,128)S(1)} %get-tuple-element.10.scale_ref), custom_call_target="tpu_custom_call" | custom-call | flops 1056964608 | bytes 33030144 | tf_op jit(solution)/shard_map/pallas_call | solution.py:269
Async XLA Ops:
  0.0 0.7 %copy-start = (bf16[2,6144]{1,0:T(2,128)(2,1)S(1)}, bf16[2,6144]{1,0:T(2,128)(2,1)}, u32[]{:S(2)}) copy-start(bf16[2,6144]{1,0:T(2,128)(2,1)} %act_ref.1) | copy-start | bytes 73732
  0.7 0.7 %copy-start.1 = (bf16[2,6144]{1,0:T(2,128)(2,1)S(1)}, bf16[2,6144]{1,0:T(2,128)(2,1)}, u32[]{:S(2)}) copy-start(bf16[2,6144]{1,0:T(2,128)(2,1)} %grad_ref.1) | copy-start | bytes 73732
  1.5 0.7 %copy-start.2 = (s32[2,4]{1,0:T(2,128)S(1)}, s32[2,4]{1,0:T(2,128)}, u32[]{:S(2)}) copy-start(s32[2,4]{1,0:T(2,128)} %ids_ref.1) | copy-start | bytes 100
  2.2 0.7 %copy-start.3 = (f32[2,4]{1,0:T(2,128)S(1)}, f32[2,4]{1,0:T(2,128)}, u32[]{:S(2)}) copy-start(f32[2,4]{1,0:T(2,128)} %score_ref.1) | copy-start | bytes 100

commit v3 on v2

--- a/solution.py
+++ b/solution.py
@@ -60,7 +60,7 @@
         for copy in weights(i, i):
             copy.start()
 
-    early, middle = min(2, slots), min(5, slots)
+    early, middle = min(2, slots), min(4, slots)
     each(0, early, start_weights)
 
     barrier = pltpu.get_barrier_semaphore()
@@ -93,18 +93,24 @@
     act_forward(0).start()
     each(1, chips, lambda k: act_copy(k).start())
 
-    score = score_ref[...]
-    share = score / jnp.sum(score, axis=1, keepdims=True)
-    ids = ids_ref[...]
     grad = to_rows(grad_ref[...].astype(jnp.float32))
     row_token = lax.broadcasted_iota(jnp.int32, (block, 1), 0) // segments
+
+    def of_row(ref, k, zero):
+        value = jnp.full((block, 1), zero)
+        for token in range(tok_rows):
+            value = jnp.where(row_token == token, ref[token, k], value)
+        return value
+
+    top = ids_ref.shape[1]
+    ids = [of_row(ids_ref, k, jnp.int32(0)) for k in range(top)]
+    score = [of_row(score_ref, k, jnp.float32(0)) for k in range(top)]
+    whole = sum(score[1:], score[0])
+    share = [value / whole for value in score]
     for index in range(EXPERTS):
-        weight = jnp.sum(jnp.where(ids == index, share, 0.0), axis=1, keepdims=True)
+        weight = sum(jnp.where(ids[k] == index, share[k], 0.0) for k in range(top))
         weight = weight.astype(jnp.bfloat16).astype(jnp.float32)
-        spread = jnp.zeros((block, 1), jnp.float32)
-        for token in range(tok_rows):
-            spread = jnp.where(row_token == token, weight[token:token + 1, :], spread)
-        scaled = (grad * spread).astype(jnp.bfloat16).astype(jnp.float32)
+        scaled = (grad * weight).astype(jnp.bfloat16).astype(jnp.float32)
         gsend[index] = (scaled * scaled).astype(jnp.bfloat16)
     gbuf[me] = gsend[me // (devices // EXPERTS)]
 
@@ -222,12 +228,13 @@
     tokens = devices * tok_rows
     segments = width // LANES
     block = tok_rows * segments
-    chunk = chunk_of(rows, 128)
+    chunk = chunk_of(rows, 192)
     chunks = rows // chunk
-    slots = min(10, chunks)
+    slots = min(7, chunks)
     chips = devices // 2
     vmem = pl.BlockSpec(memory_space=pltpu.VMEM)
     anywhere = pl.BlockSpec(memory_space=pl.ANY)
+    smem = pl.BlockSpec(memory_space=pltpu.SMEM)
     dma = pltpu.SemaphoreType.DMA
     bf16, f32 = jnp.bfloat16, jnp.float32
     hsq, gsq, scale = pl.pallas_call(
@@ -237,7 +244,7 @@
             jax.ShapeDtypeStruct((tokens, width), bf16),
             jax.ShapeDtypeStruct((8, LANES), f32),
         ),
-        in_specs=[anywhere, anywhere, vmem, vmem, vmem, vmem],
+        in_specs=[anywhere, anywhere, vmem, vmem, smem, smem],
         out_specs=(vmem, vmem, vmem),
         scratch_shapes=[
             pltpu.VMEM((slots, 2 * chunk, width), bf16),

time: 58.5 us -> 58.1 us (level)
  no operation moved by 1% of the time
where the time goes in v3:
time: 58.1 us; the launch traced here: 57.8 us
  Pallas kernels  55 us (95%)
  local copies, waits for them, and re-layouts  2.83 us (5%)
    pallas_call x1, Pallas kernels, per_device(): pl.pallas_call(functools.partial(hidden_kernel, devices, chunk, slots, ch...  40.7 us
    pallas_call x1, Pallas kernels, per_device(): pl.pallas_call(functools.partial(outer_kernel, 256), out_shape=jax.ShapeD...  14.2 us
    unnamed x8, local copies, waits for them, and re-layouts  2.83 us

profile of v3, /device:TPU:0, one launch (start us, length us, event | category | flops | bytes accessed | tf_op | source)
XLA Modules:
  0.0 57.8 jit_solution(17930108847421371296)
XLA Ops:
  0.0 0.0 copy-start
  0.0 0.7 %copy-done = bf16[2,6144]{1,0:T(2,128)(2,1)S(1)} copy-done((bf16[2,6144]{1,0:T(2,128)(2,1)S(1)}, bf16[2,6144]{1,0:T(2,128)(2,1)}, u32[]{:S(2)}) %copy-start) | copy-done | bytes 24600
  0.7 0.0 copy-start.1
  0.7 0.7 %copy-done.1 = bf16[2,6144]{1,0:T(2,128)(2,1)S(1)} copy-done((bf16[2,6144]{1,0:T(2,128)(2,1)S(1)}, bf16[2,6144]{1,0:T(2,128)(2,1)}, u32[]{:S(2)}) %copy-start.1) | copy-done | bytes 24600
  1.5 0.0 copy-start.2
  1.5 0.7 %copy-done.2 = s32[2,4]{1,0:T(2,128)S(1)} copy-done((s32[2,4]{1,0:T(2,128)S(1)}, s32[2,4]{1,0:T(2,128)}, u32[]{:S(2)}) %copy-start.2) | copy-done | bytes 56
  2.2 0.0 copy-start.3
  2.2 0.7 %copy-done.3 = f32[2,4]{1,0:T(2,128)S(1)} copy-done((f32[2,4]{1,0:T(2,128)S(1)}, f32[2,4]{1,0:T(2,128)}, u32[]{:S(2)}) %copy-start.3) | copy-done | bytes 56
  2.8 40.7 %shard_map.64 = (bf16[2688,32]{1,0:T(8,128)(2,1)S(1)}, bf16[32,6144]{1,0:T(8,128)(2,1)S(1)}, f32[8,128]{1,0:T(8,128)S(1)}) custom-call(bf16[2688,6144]{1,0:T(8,128)(2,1)} %gate_ref.1, bf16[2688,6144]{1,0:T(8,128)(2,1)} %up_ref.1, bf16[2,6144]{1,0:T(2,128)(2,1)S(1)} %copy-done, bf16[2,6144]{1,0:T(2,128)(2,1)S(1)} %copy-done.1, s32[2,4]{1,0:T(2,128)S(1)} %copy-done.2, ...), custom_call_target="tpu_custom_call" | custom-call | flops 2113929216 | bytes 66060288 | tf_op jit(solution)/shard_map/pallas_call | solution.py:240
  43.6 14.2 %shard_map.65 = bf16[2688,6144]{1,0:T(8,128)(2,1)} custom-call(bf16[2688,32]{1,0:T(8,128)(2,1)S(1)} %get-tuple-element.8.hsq_ref, bf16[32,6144]{1,0:T(8,128)(2,1)S(1)} %get-tuple-element.9.gsq_ref, f32[8,128]{1,0:T(8,128)S(1)} %get-tuple-element.10.scale_ref), custom_call_target="tpu_custom_call" | custom-call | flops 1056964608 | bytes 33030144 | tf_op jit(solution)/shard_map/pallas_call | solution.py:276
Async XLA Ops:
  0.0 0.7 %copy-start = (bf16[2,6144]{1,0:T(2,128)(2,1)S(1)}, bf16[2,6144]{1,0:T(2,128)(2,1)}, u32[]{:S(2)}) copy-start(bf16[2,6144]{1,0:T(2,128)(2,1)} %act_ref.1) | copy-start | bytes 73732
  0.7 0.7 %copy-start.1 = (bf16[2,6144]{1,0:T(2,128)(2,1)S(1)}, bf16[2,6144]{1,0:T(2,128)(2,1)}, u32[]{:S(2)}) copy-start(bf16[2,6144]{1,0:T(2,128)(2,1)} %grad_ref.1) | copy-start | bytes 73732
  1.5 0.7 %copy-start.2 = (s32[2,4]{1,0:T(2,128)S(1)}, s32[2,4]{1,0:T(2,128)}, u32[]{:S(2)}) copy-start(s32[2,4]{1,0:T(2,128)} %ids_ref.1) | copy-start | bytes 100
  2.2 0.7 %copy-start.3 = (f32[2,4]{1,0:T(2,128)S(1)}, f32[2,4]{1,0:T(2,128)}, u32[]{:S(2)}) copy-start(f32[2,4]{1,0:T(2,128)} %score_ref.1) | copy-start | bytes 100
